TPU v7x, 256 devices: a whole 4x4x8 slice. The times are simulated.
256 devices in a mesh: sec: 4 (over y_lo, core), tile: 64 (over x, z, y_hi).
Axes of the slice: x: 4, y: 4 (y_hi: 2, y_lo: 2; y = y_hi * 2 + y_lo), z: 8, core: 2. Of those that a mesh axis runs over, the one named last changes fastest.
Arguments:
- increments: float32 [8, 512, 96, 512], P('sec', 'tile'), may hold values from -6 to 6
- adjoint_forcing: float32 [8, 512, 96, 512], P('sec', 'tile'), may hold values from -6 to 6
- wind: float32 [8, 512, 96], P('sec', 'tile'), may hold values from -0.4 to 0.4
- coupling: float32 [512, 512], replicated, may hold values from -0.125 to 0.125
Outputs:
- model_misfit: float32 [8, 512, 96, 512], P('sec', 'tile')
- adjoint_misfit: float32 [8, 512, 96, 512], P('sec', 'tile')
All inputs are finite; a program needn't handle non-finite values.
Results may differ from a plain program's by a relative error of at most 0.0001.
Values sent between devices are 32-bit elements; how exact they have to be, the bound alone decides.
A program may use at most 128 MiB of HBM per device.

v0:
```python
import functools

import jax
import jax.numpy as jnp
from jax import lax
from jax.experimental import pallas as pl
from jax.experimental.pallas import tpu as pltpu
from jax.sharding import PartitionSpec as P

MESH = pl.DeviceIdType.MESH
STEPS = 4
DIFFUSION = 0.15


def halves(x):
    high = x.astype(jnp.bfloat16)
    return high, (x - high.astype(jnp.float32)).astype(jnp.bfloat16)


def dot(a, b):
    return jnp.dot(a, b, preferred_element_type=jnp.float32)


def when(condition):
    return (lambda f: f()) if condition is None else pl.when(condition)


def kernel(
    inc, forc, wind, coupling, model, adjoint,
    state, result, last, winds, speed, matrices, send, recv, wsend, wrecv, base_sem, out_sem, last_sem,
):
    sections, tiles = lax.axis_size("sec"), lax.axis_size("tile")
    sec, tile = lax.axis_index("sec"), lax.axis_index("tile")
    east, west = lax.rem(tile + 1, tiles), lax.rem(tile + tiles - 1, tiles)
    width, lats, size = inc.shape[1:]
    wide = width + 2 * STEPS
    has_next, has_previous = sec < sections - 1, sec > 0

    local = [
        pltpu.make_async_copy(inc.at[0], state.at[2, pl.ds(STEPS, width)], recv.at[2, STEPS]),
        pltpu.make_async_copy(forc.at[1], state.at[3, pl.ds(STEPS, width)], recv.at[3, STEPS]),
    ]
    bases = [
        pltpu.make_async_copy(source, result.at[unit], base_sem.at[unit])
        for unit, source in enumerate((inc.at[0], forc.at[1], inc.at[1], forc.at[0]))
    ]

    barrier = pltpu.get_barrier_semaphore()
    for to, condition in ((sec, None), (sec + 1, has_next), (sec - 1, has_previous)):
        for t in (east, west) if condition is None else (east, west, tile):
            @when(condition)
            def _():
                pl.semaphore_signal(barrier, inc=1, device_id=(to, t), device_id_type=MESH)

    def remote(source, target, sems, at, device):
        return pltpu.make_async_remote_copy(
            src_ref=source, dst_ref=target, send_sem=sems[0].at[at], recv_sem=sems[1].at[at],
            device_id=device, device_id_type=MESH,
        )

    def wind_copies(unit, window, section, parts):
        to = {0: east, 1: tile, 2: west}
        return [
            remote(wind.at[window], winds.at[unit, pl.ds(8 * part, 8)], (wsend, wrecv), (unit, part), (section, to[part]))
            for part in parts
        ]

    def halo(unit, source, section, part, first, count):
        if part == 0:
            at, column, to = STEPS - first - count, width - first - count, east
        else:
            at, column, to = STEPS + width + first, first, west
        return remote(
            source.at[pl.ds(column, count)], state.at[unit, pl.ds(at, count)], (send, recv), (unit, at), (section, to)
        )

    def start_of(unit, source, section):
        return remote(
            source, state.at[unit, pl.ds(STEPS, width)], (send, recv), (unit, STEPS), (section, tile)
        )

    ahead = (has_next, has_previous)
    behind = (has_previous, has_next)
    copies = []
    copies += [(c, *ahead) for c in wind_copies(0, 1, sec + 1, (1, 0, 2))]
    copies += [(c, *behind) for c in wind_copies(1, 0, sec - 1, (1, 0, 2))]
    copies += [(c, None, None) for c in wind_copies(2, 0, sec, (0, 2)) + wind_copies(3, 1, sec, (0, 2))]
    copies += [(start_of(0, inc.at[1], sec + 1), *ahead)]
    copies += [(start_of(1, forc.at[0], sec - 1), *behind)]
    copies += [(halo(0, inc.at[1], sec + 1, part, 0, STEPS), *ahead) for part in (0, 1)]
    copies += [(halo(1, forc.at[0], sec - 1, part, 0, STEPS), *behind) for part in (0, 1)]
    copies += [(halo(2, inc.at[0], sec, part, 0, STEPS), None, None) for part in (0, 1)]
    near = [[halo(3, forc.at[1], sec, part, j, 1) for part in (0, 1)] for j in range(STEPS - 1)]
    copies += [(c, None, None) for pair in near for c in pair]
    far = [
        remote(forc.at[1, column], last.at[part], (last_sem.at[0], last_sem.at[1]), part, (sec, to))
        for part, column, to in ((0, width - STEPS, east), (1, STEPS - 1, west))
    ]
    copies += [(c, None, None) for c in far]

    for c in local + bases:
        c.start()
    pl.semaphore_wait(barrier, 8 - 3 * ((sec + 1) // sections) - 3 * ((sections - sec) // sections))
    for c, sends, _ in copies:
        @when(sends)
        def _():
            c.start()

    for at, matrix in enumerate((coupling[...].T, coupling[...])):
        high, low = halves(matrix)
        matrices[2 * at] = high
        matrices[2 * at + 1] = low
    zero = jnp.zeros((lats, size), jnp.float32)
    state[3, 0] = zero
    state[3, wide - 1] = zero
    winds[2, pl.ds(8, 8)] = wind[0]
    winds[3, pl.ds(8, 8)] = wind[1]

    def active(unit):
        return jnp.logical_not(((unit == 0) & (sec == 0)) | ((unit == 1) & (sec == sections - 1)))

    def wait_wind(unit, part):
        remote(wind.at[0], winds.at[unit, pl.ds(8 * part, 8)], (wsend, wrecv), (unit, part), (sec, east)).wait_recv()

    def spread(unit, _):
        @pl.when(active(unit))
        def _():
            wait_wind(unit, 0)
            wait_wind(unit, 2)

            @pl.when(unit < 2)
            def _():
                wait_wind(unit, 1)

            turned = winds[unit].T * jnp.where(unit % 2 == 0, 1.0, -1.0)
            for column in range(wide):
                speed[unit, column] = jnp.broadcast_to(turned[:, column + 4 : column + 5], (lats, 128))
        return 0

    lax.fori_loop(0, 4, spread, 0)

    lat = lax.broadcasted_iota(jnp.int32, (lats, size), 0)

    def flow(unit, column):
        return jnp.concatenate([speed[unit, column]] * (size // 128), 1)

    def update(unit, step, column):
        base = jnp.where(unit == 3, 4 + STEPS - 1, 4)
        source = jnp.where(step == 1, unit, base + step - 2)
        shift = unit % 2
        columns = (column, wide - 1 - column)
        centre = [state[source, at] for at in columns]
        high, low = halves(jnp.concatenate(centre, 0))
        coarse, fine = matrices[2 * shift], matrices[2 * shift + 1]
        mixed = dot(high, coarse) + dot(low, coarse) + dot(high, fine)
        for i, at in enumerate(columns):
            x = centre[i]
            north = jnp.where(lat == lats - 1, 0.0, pltpu.roll(x, lats - 1, 0))
            south = jnp.where(lat == 0, 0.0, pltpu.roll(x, 1, 0))
            value = (
                (1 - 2 * DIFFUSION) * x
                + mixed[i * lats : (i + 1) * lats]
                + flow(unit, at - shift) * state[source, at - 1]
                - flow(unit, at + shift) * state[source, at + 1]
                + DIFFUSION * (north + south)
            )

            @pl.when(step < STEPS)
            def _():
                state[base + step - 1, at] = value

            @pl.when(step == STEPS)
            def _():
                result[unit, at - STEPS] -= value

    def outgoing(unit):
        target = (model.at[0], adjoint.at[1], model.at[1], adjoint.at[0])[unit]
        return pltpu.make_async_copy(result.at[unit], target, out_sem.at[unit])

    local[1].wait()
    half = wide // 2

    def inner(step, _):
        def columns(column, _):
            update(3, step, column)
            return 0

        return lax.fori_loop(STEPS + step, half, columns, 0)

    lax.fori_loop(1, STEPS, inner, 0)
    for c in bases:
        c.wait()

    def whole(unit, _):
        @pl.when(active(unit))
        def _():
            for at, count in ((STEPS, width), (0, STEPS), (STEPS + width, STEPS)):
                remote(
                    inc.at[0, pl.ds(0, count)], state.at[unit, pl.ds(at, count)], (send, recv), (unit, at), (sec, east)
                ).wait_recv()

            def steps(step, _):
                def columns(column, _):
                    update(unit, step, column)
                    return 0

                return lax.fori_loop(step, half, columns, 0)

            lax.fori_loop(1, STEPS + 1, steps, 0)

        return 0

    lax.fori_loop(0, 3, whole, 0)
    for unit in range(3):
        outgoing(unit).start()

    def waves(j, _):
        @pl.when(j < STEPS)
        def _():
            for at in (STEPS - j, STEPS + width - 1 + j):
                remote(
                    forc.at[1, pl.ds(0, 1)], state.at[3, pl.ds(at, 1)], (send, recv), (3, at), (sec, east)
                ).wait_recv()

        def steps(step, _):
            update(3, step, STEPS - j + step)
            return 0

        return lax.fori_loop(1, STEPS + 1, steps, 0)

    lax.fori_loop(1, STEPS + 1, waves, 0)

    for part in (0, 1):
        reach = functools.reduce(
            jnp.multiply, [flow(3, step - 1 if part == 0 else wide - step) for step in range(1, STEPS + 1)]
        )
        far[part].wait_recv()
        result[3, 0 if part == 0 else width - 1] -= reach * last[part]
    outgoing(3).start()

    for c, sends, _ in copies:
        @when(sends)
        def _():
            c.wait_send()
    for unit in range(4):
        outgoing(unit).wait()


def solution(mesh):
    def body(increments, adjoint_forcing, wind, coupling):
        _, width, lats, size = increments.shape
        wide = width + 2 * STEPS
        any_space = pl.BlockSpec(memory_space=pl.ANY)
        vmem = pl.BlockSpec(memory_space=pltpu.VMEM)
        shape = jax.ShapeDtypeStruct(increments.shape, jnp.float32)
        return pl.pallas_call(
            kernel,
            out_shape=(shape, shape),
            in_specs=[any_space, any_space, vmem, vmem],
            out_specs=(any_space, any_space),
            scratch_shapes=[
                pltpu.VMEM((4 + 2 * (STEPS - 1), wide, lats, size), jnp.float32),
                pltpu.VMEM((4, width, lats, size), jnp.float32),
                pltpu.VMEM((2, lats, size), jnp.float32),
                pltpu.VMEM((4, 3 * width, lats), jnp.float32),
                pltpu.VMEM((4, wide, lats, 128), jnp.float32),
                pltpu.VMEM((4, size, size), jnp.bfloat16),
                pltpu.SemaphoreType.DMA((4, wide)),
                pltpu.SemaphoreType.DMA((4, wide)),
                pltpu.SemaphoreType.DMA((4, 3)),
                pltpu.SemaphoreType.DMA((4, 3)),
                pltpu.SemaphoreType.DMA((4,)),
                pltpu.SemaphoreType.DMA((4,)),
                pltpu.SemaphoreType.DMA((2, 2)),
            ],
            compiler_params=pltpu.CompilerParams(
                collective_id=0, has_side_effects=True, vmem_limit_bytes=56 * 2**20
            ),
        )(increments, adjoint_forcing, wind, coupling)

    in_specs = (
        P("sec", "tile", None, None),
        P("sec", "tile", None, None),
        P("sec", "tile", None),
        P(),
    )
    out_specs = (P("sec", "tile", None, None), P("sec", "tile", None, None))
    return jax.shard_map(body, mesh=mesh, in_specs=in_specs, out_specs=out_specs, check_vma=False)
```

profile of v0, /device:TPU:16, one launch (start us, length us, event | category | flops | bytes accessed | tf_op | source)
XLA Modules:
  0.0 168.4 jit_solution(849022995247106979)
XLA Ops:
  0.6 162.0 %shard_map.59 = (f32[2,8,96,512]{3,2,1,0:T(8,128)}, f32[2,8,96,512]{3,2,1,0:T(8,128)}) custom-call(f32[2,8,96,512]{3,2,1,0:T(8,128)} %inc.1, f32[2,8,96,512]{3,2,1,0:T(8,128)} %forc.1, f32[2,8,96]{2,1,0:T(8,128)} %wind.1, f32[512,512]{1,0:T(8,128)} %coupling.1), custom_call_target="tpu_custom_call" | custom-call | tf_op jit(solution)/shard_map/pallas_call | solution.py:256
  162.6 0.0 copy-start
  162.6 4.1 %copy.8 = f32[2,8,96,512]{3,2,1,0:T(8,128)} copy(f32[2,8,96,512]{3,2,1,0:T(8,128)} %get-tuple-element.4) | data formatting | bytes 6291456
  166.7 0.0 copy-done
  166.7 1.7 copy.9
Async XLA Ops:
  162.6 4.1 %copy-start = (f32[2,8,96,512]{3,2,1,0:T(8,128)S(1)}, f32[2,8,96,512]{3,2,1,0:T(8,128)}, u32[]{:S(2)}) copy-start(f32[2,8,96,512]{3,2,1,0:T(8,128)} %get-tuple-element.5) | copy-start | bytes 9437188
where the time goes:
time: 169 us; the launch traced here: 168 us
  Pallas kernels  162 us (96%)
  local copies, waits for them, and re-layouts  5.79 us (3%)
    pallas_call x1, Pallas kernels, body(): pl.pallas_call(kernel, out_shape=(shape, shape), in_specs=[any_space, any...  162 us
    unnamed x4, local copies, waits for them, and re-layouts  5.79 us

commit v1 on v0

v1 whole, which is shorter than its diff:
```python
import functools

import jax
import jax.numpy as jnp
from jax import lax
from jax.experimental import pallas as pl
from jax.experimental.pallas import tpu as pltpu
from jax.sharding import PartitionSpec as P

MESH = pl.DeviceIdType.MESH
STEPS = 4
DIFFUSION = 0.15
FIRST = 12
LATER = ((0, (12, 13)), (1, (14, 15)))


def level(step):
    return 15 * step - step * (step - 1)


def halves(x):
    high = x.astype(jnp.bfloat16)
    return high, (x - high.astype(jnp.float32)).astype(jnp.bfloat16)


def dot(a, b):
    return jnp.dot(a, b, preferred_element_type=jnp.float32)


def when(condition):
    return (lambda f: f()) if condition is None else pl.when(condition)


def kernel(
    inc, forc, wind, coupling, model, adjoint,
    state, result, last, winds, speed, matrices, send, recv, wsend, wrecv, base_sem, out_sem, last_sem,
):
    sections, tiles = lax.axis_size("sec"), lax.axis_size("tile")
    sec, tile = lax.axis_index("sec"), lax.axis_index("tile")
    east, west = lax.rem(tile + 1, tiles), lax.rem(tile + tiles - 1, tiles)
    width, lats, size = inc.shape[1:]
    wide = width + 2 * STEPS
    has_next, has_previous = sec < sections - 1, sec > 0

    local = [
        pltpu.make_async_copy(source.at[pl.ds(at, 2)], state.at[unit, pl.ds(STEPS + at, 2)], recv.at[unit, STEPS + at])
        for unit, source in ((0, inc.at[0]), (3, forc.at[1]))
        for at in range(0, width, 2)
    ]
    bases = [
        pltpu.make_async_copy(source, result.at[unit], base_sem.at[unit])
        for unit, source in enumerate((inc.at[1], forc.at[1], inc.at[0], forc.at[0]))
    ]

    barrier = pltpu.get_barrier_semaphore()
    for to, condition in ((sec, None), (sec + 1, has_next), (sec - 1, has_previous)):
        for t in (east, west) if condition is None else (east, west, tile):
            @when(condition)
            def _():
                pl.semaphore_signal(barrier, inc=1, device_id=(to, t), device_id_type=MESH)

    def remote(source, target, sems, at, device):
        return pltpu.make_async_remote_copy(
            src_ref=source, dst_ref=target, send_sem=sems[0].at[at], recv_sem=sems[1].at[at],
            device_id=device, device_id_type=MESH,
        )

    def wind_copies(unit, window, section, parts):
        to = {0: east, 1: tile, 2: west}
        return [
            remote(wind.at[window], winds.at[unit, pl.ds(8 * part, 8)], (wsend, wrecv), (unit, part), (section, to[part]))
            for part in parts
        ]

    def halo(unit, source, section, part, first, count):
        if part == 0:
            at, column, to = STEPS - first - count, width - first - count, east
        else:
            at, column, to = STEPS + width + first, first, west
        return remote(
            source.at[pl.ds(column, count)], state.at[unit, pl.ds(at, count)], (send, recv), (unit, at), (section, to)
        )

    def start_of(unit, source, section, at):
        return remote(
            source.at[pl.ds(at, 2)], state.at[unit, pl.ds(STEPS + at, 2)], (send, recv), (unit, STEPS + at), (section, tile)
        )

    def pair(unit, j):
        source, to, sends = (
            (inc.at[0], sec, None), (forc.at[0], sec - 1, has_previous), (inc.at[1], sec + 1, has_next), (forc.at[1], sec, None)
        )[unit]
        return [(halo(unit, source, to, part, j - 1, 1), sends) for part in (0, 1)]

    def far(at):
        source = (inc.at[0], forc.at[1])[at]
        return [
            (remote(source.at[column], last.at[at, part], (last_sem.at[0], last_sem.at[1]), (at, part), (sec, to)), None)
            for part, column, to in ((0, width - STEPS, east), (1, STEPS - 1, west))
        ]

    small = [(c, None) for c in wind_copies(0, 0, sec, (0, 2)) + wind_copies(3, 1, sec, (0, 2))]
    small += [(c, has_previous) for c in wind_copies(1, 0, sec - 1, (1, 0, 2))]
    small += [(c, has_next) for c in wind_copies(2, 1, sec + 1, (1, 0, 2))]
    starts = [
        [(start_of(1, forc.at[0], sec - 1, at), has_previous), (start_of(2, inc.at[1], sec + 1, at), has_next)]
        for at in range(0, width, 2)
    ]
    order = [(unit, j) for j in range(1, STEPS + 1) for unit in (1, 2)]
    order += [(unit, j) for j in range(1, STEPS) for unit in (0, 3)]
    farthest = [far(0), far(1)]
    pairs = [pair(unit, j) for unit, j in order] + farthest

    def launch(group):
        for c, sends in group:
            @when(sends)
            def _():
                c.start()

    def leave(group):
        for c, sends in group:
            @when(sends)
            def _():
                c.wait_send()

    for c in local + bases:
        c.start()
    pl.semaphore_wait(barrier, 8 - 3 * ((sec + 1) // sections) - 3 * ((sections - sec) // sections))
    launch(small)
    for at, group in enumerate(pairs[:FIRST]):
        if at % 2 == 0 and at // 2 < len(starts):
            launch(starts[at // 2])
        launch(group)

    for at, matrix in enumerate((coupling[...].T, coupling[...])):
        high, low = halves(matrix)
        matrices[2 * at] = high
        matrices[2 * at + 1] = low
    zero = jnp.zeros((lats, size), jnp.float32)
    for unit in (0, 3):
        state[unit, 0] = zero
        state[unit, wide - 1] = zero
    winds[0, pl.ds(8, 8)] = wind[0]
    winds[3, pl.ds(8, 8)] = wind[1]

    def active(unit):
        return jnp.logical_not(((unit == 1) & (sec == sections - 1)) | ((unit == 2) & (sec == 0)))

    def wait_wind(unit, part):
        remote(wind.at[0], winds.at[unit, pl.ds(8 * part, 8)], (wsend, wrecv), (unit, part), (sec, east)).wait_recv()

    def spread(unit, _):
        @pl.when(active(unit))
        def _():
            wait_wind(unit, 0)
            wait_wind(unit, 2)

            @pl.when((unit == 1) | (unit == 2))
            def _():
                wait_wind(unit, 1)

            turned = winds[unit].T * jnp.where(unit % 2 == 0, 1.0, -1.0)
            for column in range(wide):
                speed[unit, column] = jnp.broadcast_to(turned[:, column + 4 : column + 5], (lats, 128))
        return 0

    lax.fori_loop(0, 4, spread, 0)

    lat = lax.broadcasted_iota(jnp.int32, (lats, size), 0)

    def flow(unit, column):
        return jnp.concatenate([speed[unit, column]] * (size // 128), 1)

    def update(units, step, column):
        before, after = level(step - 1), level(step)
        columns = (column, wide - 1 - column)
        centres = [[state[unit, before + at] for at in columns] for unit in units]
        mixed = []
        for way, centre in enumerate(centres):
            high, low = halves(jnp.concatenate(centre, 0))
            coarse, fine = matrices[2 * way], matrices[2 * way + 1]
            mixed.append(dot(high, coarse) + dot(low, coarse) + dot(high, fine))
        values = []
        for way, unit in enumerate(units):
            for i, at in enumerate(columns):
                x = centres[way][i]
                north = jnp.where(lat == lats - 1, 0.0, pltpu.roll(x, lats - 1, 0))
                south = jnp.where(lat == 0, 0.0, pltpu.roll(x, 1, 0))
                value = (
                    (1 - 2 * DIFFUSION) * x
                    + mixed[way][i * lats : (i + 1) * lats]
                    + flow(unit, at - way) * state[unit, before + at - 1]
                    - flow(unit, at + way) * state[unit, before + at + 1]
                    + DIFFUSION * (north + south)
                )
                values.append((unit, at, value))

        @pl.when(step < STEPS)
        def _():
            for unit, at, value in values:
                state[unit, after + at] = value

        @pl.when(step == STEPS)
        def _():
            for unit, at, value in values:
                result[unit, at - STEPS] -= jnp.where(active(unit), value, 0.0)

    def outgoing(unit):
        target = (model.at[1], adjoint.at[1], model.at[0], adjoint.at[0])[unit]
        return pltpu.make_async_copy(result.at[unit], target, out_sem.at[unit])

    for c in bases:
        c.wait()
    half = wide // 2

    def arrive(unit, at, count):
        remote(
            inc.at[0, pl.ds(0, count)], state.at[unit, pl.ds(at, count)], (send, recv), (unit, at), (sec, east)
        ).wait_recv()

    def event(number, _):
        moved = (number >= 1) & (number <= STEPS)
        units = (jnp.where(moved, 2, 0), jnp.where(moved, 1, 3))
        j = jnp.where(number > STEPS, number - STEPS, number)
        opens = number <= 1
        for unit in units:
            @pl.when(active(unit))
            def _():
                @pl.when(opens)
                def _():
                    for at in range(STEPS, STEPS + width, 2):
                        arrive(unit, at, 2)

                @pl.when((j > 0) & (number < 2 * STEPS))
                def _():
                    arrive(unit, STEPS - j, 1)
                    arrive(unit, STEPS + width - 1 + j, 1)

        for at, numbers in LATER:
            @pl.when(number == at + 1)
            def _():
                for follower in numbers:
                    launch(pairs[follower])

        def wave(q, _):
            def steps(step, _):
                def columns(column, _):
                    update(units, step, column)
                    return 0

                first = STEPS - q + step
                return lax.fori_loop(first, jnp.where(q == 0, half, first + 1), columns, 0)

            return lax.fori_loop(1, STEPS + 1, steps, 0)

        lax.fori_loop(jnp.where(opens, 0, j), j + 1, wave, 0)

        @pl.when(number == STEPS)
        def _():
            outgoing(1).start()
            outgoing(2).start()

        return 0

    lax.fori_loop(0, 2 * STEPS + 1, event, 0)

    for at, unit in enumerate((0, 3)):
        for part in (0, 1):
            first = -at if part == 0 else at
            reach = functools.reduce(
                jnp.multiply, [flow(unit, (step if part == 0 else wide - 1 - step) + first) for step in range(1, STEPS + 1)]
            )
            farthest[at][part][0].wait_recv()
            result[unit, 0 if part == 0 else width - 1] -= reach * last[at, part]
        outgoing(unit).start()

    for group in [small, *starts, *pairs]:
        leave(group)
    for unit in range(4):
        outgoing(unit).wait()


def solution(mesh):
    def body(increments, adjoint_forcing, wind, coupling):
        _, width, lats, size = increments.shape
        wide = width + 2 * STEPS
        any_space = pl.BlockSpec(memory_space=pl.ANY)
        vmem = pl.BlockSpec(memory_space=pltpu.VMEM)
        shape = jax.ShapeDtypeStruct(increments.shape, jnp.float32)
        return pl.pallas_call(
            kernel,
            out_shape=(shape, shape),
            in_specs=[any_space, any_space, vmem, vmem],
            out_specs=(any_space, any_space),
            scratch_shapes=[
                pltpu.VMEM((4, level(STEPS - 1) + wide - STEPS + 1, lats, size), jnp.float32),
                pltpu.VMEM((4, width, lats, size), jnp.float32),
                pltpu.VMEM((2, 2, lats, size), jnp.float32),
                pltpu.VMEM((4, 3 * width, lats), jnp.float32),
                pltpu.VMEM((4, wide, lats, 128), jnp.float32),
                pltpu.VMEM((4, size, size), jnp.bfloat16),
                pltpu.SemaphoreType.DMA((4, wide)),
                pltpu.SemaphoreType.DMA((4, wide)),
                pltpu.SemaphoreType.DMA((4, 3)),
                pltpu.SemaphoreType.DMA((4, 3)),
                pltpu.SemaphoreType.DMA((4,)),
                pltpu.SemaphoreType.DMA((4,)),
                pltpu.SemaphoreType.DMA((2, 2, 2)),
            ],
            compiler_params=pltpu.CompilerParams(
                collective_id=0, has_side_effects=True, vmem_limit_bytes=58 * 2**20
            ),
        )(increments, adjoint_forcing, wind, coupling)

    in_specs = (
        P("sec", "tile", None, None),
        P("sec", "tile", None, None),
        P("sec", "tile", None),
        P(),
    )
    out_specs = (P("sec", "tile", None, None), P("sec", "tile", None, None))
    return jax.shard_map(body, mesh=mesh, in_specs=in_specs, out_specs=out_specs, check_vma=False)
```

time: 169 us -> 157 us (0.929)
  the two profiles are of different devices: /device:TPU:16 before, /device:TPU:1 now
where the time goes in v1:
time: 157 us
  Pallas kernels  151 us (96%)
  local copies, waits for them, and re-layouts  5.79 us (4%)
    pallas_call x1, Pallas kernels, body(): pl.pallas_call(kernel, out_shape=(shape, shape), in_specs=[any_space, any...  151 us
    unnamed x4, local copies, waits for them, and re-layouts  5.79 us

profile of v1, /device:TPU:1, one launch (start us, length us, event | category | flops | bytes accessed | tf_op | source)
XLA Modules:
  0.0 157.2 jit_solution(1153982633793614389)
XLA Ops:
  0.6 150.7 %shard_map.59 = (f32[2,8,96,512]{3,2,1,0:T(8,128)}, f32[2,8,96,512]{3,2,1,0:T(8,128)}) custom-call(f32[2,8,96,512]{3,2,1,0:T(8,128)} %inc.1, f32[2,8,96,512]{3,2,1,0:T(8,128)} %forc.1, f32[2,8,96]{2,1,0:T(8,128)} %wind.1, f32[512,512]{1,0:T(8,128)} %coupling.1), custom_call_target="tpu_custom_call" | custom-call | tf_op jit(solution)/shard_map/pallas_call | solution.py:290
  151.4 0.0 copy-start
  151.4 4.1 %copy.8 = f32[2,8,96,512]{3,2,1,0:T(8,128)} copy(f32[2,8,96,512]{3,2,1,0:T(8,128)} %get-tuple-element.4) | data formatting | bytes 6291456
  155.5 0.0 copy-done
  155.5 1.7 %copy.9 = f32[2,8,96,512]{3,2,1,0:T(8,128)} copy(f32[2,8,96,512]{3,2,1,0:T(8,128)S(1)} %copy-done) | data formatting | bytes 6291456
Async XLA Ops:
  151.4 4.1 %copy-start = (f32[2,8,96,512]{3,2,1,0:T(8,128)S(1)}, f32[2,8,96,512]{3,2,1,0:T(8,128)}, u32[]{:S(2)}) copy-start(f32[2,8,96,512]{3,2,1,0:T(8,128)} %get-tuple-element.5) | copy-start | bytes 9437188

commit v2 on v1

--- a/solution.py
+++ b/solution.py
@@ -10,8 +10,8 @@
 MESH = pl.DeviceIdType.MESH
 STEPS = 4
 DIFFUSION = 0.15
-FIRST = 12
-LATER = ((0, (12, 13)), (1, (14, 15)))
+FIRST = 10
+LATER = ((0, (10, 11, 12, 13)), (1, (14, 15)))
 
 
 def level(step):

time: 157 us -> 153 us (0.975)
  Pallas kernels: 151 us -> 146 us
    pallas_call x1, Pallas kernels: 151 us -> 146 us  [body(): pl.pallas_call(kernel, out_shape=(shape, shape), in_specs=[any_space, any...]
where the time goes in v2:
time: 153 us
  Pallas kernels  146 us (95%)
  local copies, waits for them, and re-layouts  5.79 us (4%)
    pallas_call x1, Pallas kernels, body(): pl.pallas_call(kernel, out_shape=(shape, shape), in_specs=[any_space, any...  146 us
    unnamed x4, local copies, waits for them, and re-layouts  5.79 us

profile of v2, /device:TPU:1, one launch (start us, length us, event | category | flops | bytes accessed | tf_op | source)
XLA Modules:
  0.0 152.5 jit_solution(3206344391525167137)
XLA Ops:
  0.6 146.1 %shard_map.59 = (f32[2,8,96,512]{3,2,1,0:T(8,128)}, f32[2,8,96,512]{3,2,1,0:T(8,128)}) custom-call(f32[2,8,96,512]{3,2,1,0:T(8,128)} %inc.1, f32[2,8,96,512]{3,2,1,0:T(8,128)} %forc.1, f32[2,8,96]{2,1,0:T(8,128)} %wind.1, f32[512,512]{1,0:T(8,128)} %coupling.1), custom_call_target="tpu_custom_call" | custom-call | tf_op jit(solution)/shard_map/pallas_call | solution.py:290
  146.7 0.0 copy-start
  146.7 4.1 %copy.8 = f32[2,8,96,512]{3,2,1,0:T(8,128)} copy(f32[2,8,96,512]{3,2,1,0:T(8,128)} %get-tuple-element.4) | data formatting | bytes 6291456
  150.9 0.0 copy-done
  150.9 1.7 %copy.9 = f32[2,8,96,512]{3,2,1,0:T(8,128)} copy(f32[2,8,96,512]{3,2,1,0:T(8,128)S(1)} %copy-done) | data formatting | bytes 6291456
Async XLA Ops:
  146.7 4.1 %copy-start = (f32[2,8,96,512]{3,2,1,0:T(8,128)S(1)}, f32[2,8,96,512]{3,2,1,0:T(8,128)}, u32[]{:S(2)}) copy-start(f32[2,8,96,512]{3,2,1,0:T(8,128)} %get-tuple-element.5) | copy-start | bytes 9437188
